TPU v7x, 256 devices: a whole 4x4x8 slice. The times are simulated.
256 devices in a mesh: pipe: 16 (over x_lo, y, core), expert: 8 (over z), dp: 2 (over x_hi).
Axes of the slice: x: 4 (x_hi: 2, x_lo: 2; x = x_hi * 2 + x_lo), y: 4, z: 8, core: 2. Of those that a mesh axis runs over, the one named last changes fastest.
Arguments:
- fwd_in: bfloat16 [16, 2048, 3584], P('pipe', ('expert', 'dp')), may hold values from -6 to 6
- fwd_ids: int32 [16, 2048, 1], P('pipe', ('expert', 'dp')), may hold values from 0 to 3; in each aligned block of 128 rows (0 to 127, 128 to 255, ..., all dimensions but the last counted through in order) at most 40 rows name the same one
- fwd_gates: float32 [16, 2048, 1], P('pipe', ('expert', 'dp')), may hold values from 0.2 to 1
- bwd_in: bfloat16 [16, 2048, 3584], P('pipe', ('expert', 'dp')), may hold values from -6 to 6
- bwd_grad: bfloat16 [16, 2048, 3584], P('pipe', ('expert', 'dp')), may hold values from -6 to 6
- bwd_ids: int32 [16, 2048, 1], P('pipe', ('expert', 'dp')), may hold values from 0 to 3; in each aligned block of 128 rows (0 to 127, 128 to 255, ..., all dimensions but the last counted through in order) at most 40 rows name the same one
- bwd_gates: float32 [16, 2048, 1], P('pipe', ('expert', 'dp')), may hold values from 0.2 to 1
- gate_w: bfloat16 [16, 3584, 4096], P('pipe', 'dp', 'expert'), may hold values from -0.09375 to 0.09375
- up_w: bfloat16 [16, 3584, 4096], P('pipe', 'dp', 'expert'), may hold values from -0.09375 to 0.09375
- down_w: bfloat16 [16, 3584, 4096], P('pipe', 'dp', 'expert'), may hold values from -0.1875 to 0.1875
Outputs:
- fwd_next: bfloat16 [16, 2048, 3584], P('pipe', ('expert', 'dp'))
- bwd_next: bfloat16 [16, 2048, 3584], P('pipe', ('expert', 'dp'))
- gate_grad: bfloat16 [16, 3584, 4096], P('pipe', 'dp', 'expert')
Inputs may be any that keep to these rules, and one draw needn't show every extreme that they name: `fwd_ids`: at every section the 128 tokens of one routing block (aligned blocks of rows) name any expert at most 40 times, a bound that some block reaches; each token names exactly 1 expert. `bwd_ids`: as for fwd_ids.
All inputs are finite; a program needn't handle non-finite values.
Results may differ from a plain program's by a relative error of at most 0.01.
Values may be sent and summed in bfloat16 or wider, within the bound.
A program may use at most 128 MiB of HBM per device.

v0:
```python
import jax
import jax.numpy as jnp
from jax import lax
from jax.sharding import PartitionSpec as P

SPLIT = 2


def shifted(block, axis, distance):
    devices = range(lax.axis_size(axis))
    route = [((i - distance) % len(devices), i) for i in devices]
    return lax.ppermute(block, axis, route)


def slot_index(ids, experts, capacity):
    flat = ids.reshape(-1)
    onehot = (flat[:, None] == jnp.arange(experts, dtype=jnp.int32)[None, :]).astype(jnp.int32)
    ranked = jnp.sum(onehot * (jnp.cumsum(onehot, axis=0) - 1), axis=1)
    return flat * capacity + ranked


def dispatch(rows, index, experts, capacity):
    empty = jnp.zeros((experts * capacity, rows.shape[1]), rows.dtype)
    placed = empty.at[index].set(rows).reshape(experts, capacity, rows.shape[1])
    return jnp.repeat(placed, SPLIT, axis=0)


def merge_halves(returned, experts):
    shape = returned.shape
    parts = returned.reshape(experts, SPLIT, shape[1], shape[2]).astype(jnp.float32)
    return jnp.sum(parts, axis=1)


def collect(output, index, gates, base):
    picked = output.reshape(-1, output.shape[2])[index].reshape(gates.shape[0], gates.shape[1], -1)
    total = base.astype(jnp.float32) + jnp.sum(gates[:, :, None] * picked, axis=1)
    return total.astype(jnp.bfloat16)


def expert_forward(received, w_gate, w_up, w_down):
    shape = received.shape
    rows = received.reshape(-1, shape[2])
    gate_pre = jnp.dot(rows, w_gate, preferred_element_type=jnp.float32)
    up_pre = jnp.dot(rows, w_up, preferred_element_type=jnp.float32)
    hidden = (jax.nn.silu(gate_pre) * up_pre).astype(jnp.bfloat16)
    output = lax.dot_general(
        hidden, w_down, (((1,), (1,)), ((), ())), preferred_element_type=jnp.float32
    )
    return output.astype(jnp.bfloat16).reshape(shape)


def expert_backward(x_recv, z_recv, w_gate, w_up, w_down):
    shape = x_recv.shape
    x_rows = x_recv.reshape(-1, shape[2])
    z_rows = z_recv.reshape(-1, shape[2])
    gate_pre = jnp.dot(x_rows, w_gate, preferred_element_type=jnp.float32)
    up_pre = jnp.dot(x_rows, w_up, preferred_element_type=jnp.float32)
    sigma = jax.nn.sigmoid(gate_pre)
    active = gate_pre * sigma
    d_hidden = jnp.dot(z_rows, w_down, preferred_element_type=jnp.float32)
    d_gate = (d_hidden * up_pre * sigma * (1.0 + gate_pre * (1.0 - sigma))).astype(jnp.bfloat16)
    d_up = (d_hidden * active).astype(jnp.bfloat16)
    contract = (((1,), (1,)), ((), ()))
    back = lax.dot_general(d_gate, w_gate, contract, preferred_element_type=jnp.float32)
    back = back + lax.dot_general(d_up, w_up, contract, preferred_element_type=jnp.float32)
    inner = (shape[0], shape[1], w_gate.shape[1])
    return (back.astype(jnp.bfloat16).reshape(shape), d_gate.reshape(inner))


def per_device(
    fwd_in, fwd_ids, fwd_gates, bwd_in, bwd_grad, bwd_ids, bwd_gates, gate_w, up_w, down_w
):
    holders = lax.axis_size("expert")
    experts = holders // SPLIT
    w_gate, w_up, w_down = (
        lax.all_gather(gate_w[0], "dp", axis=0, tiled=True),
        lax.all_gather(up_w[0], "dp", axis=0, tiled=True),
        lax.all_gather(down_w[0], "dp", axis=0, tiled=True),
    )
    f_rows = fwd_in[0]
    x_rows_in = bwd_in[0]
    g_rows = bwd_grad[0]
    row_count = f_rows.shape[0]
    features = f_rows.shape[1]
    picks = fwd_ids.shape[2]
    capacity = min(row_count, row_count * picks * 5 // (4 * experts))
    f_index = slot_index(fwd_ids[0], experts, capacity)
    f_buf = dispatch(jnp.repeat(f_rows, picks, axis=0), f_index, experts, capacity)
    b_index = slot_index(bwd_ids[0], experts, capacity)
    scaled = (bwd_gates[0][:, :, None] * g_rows[:, None, :].astype(jnp.float32)).astype(
        jnp.bfloat16
    )
    x_buf = dispatch(jnp.repeat(x_rows_in, picks, axis=0), b_index, experts, capacity)
    z_buf = dispatch(scaled.reshape(-1, features), b_index, experts, capacity)
    received = lax.all_to_all(f_buf, "expert", split_axis=0, concat_axis=0, tiled=True)
    f_back = lax.all_to_all(
        expert_forward(received, w_gate, w_up, w_down),
        "expert",
        split_axis=0,
        concat_axis=0,
        tiled=True,
    )
    x_recv, z_recv = (
        lax.all_to_all(x_buf, "expert", split_axis=0, concat_axis=0, tiled=True),
        lax.all_to_all(z_buf, "expert", split_axis=0, concat_axis=0, tiled=True),
    )
    back, d_gate = expert_backward(x_recv, z_recv, w_gate, w_up, w_down)
    b_back = lax.all_to_all(back, "expert", split_axis=0, concat_axis=0, tiled=True)
    layer_out = collect(merge_halves(f_back, experts), f_index, fwd_gates[0], f_rows)
    input_grad = collect(
        merge_halves(b_back, experts), b_index, jnp.ones_like(bwd_gates[0]), g_rows
    )
    fwd_next = shifted(layer_out[None], "pipe", 1)
    bwd_next = shifted(input_grad[None], "pipe", -1)
    hidden_units = w_gate.shape[1]
    x_rows = x_recv.reshape(-1, features)
    gate_rows = d_gate.reshape(-1, hidden_units)
    contract = (((0,), (0,)), ((), ()))
    summed = lax.psum_scatter(
        lax.dot_general(x_rows, gate_rows, contract, preferred_element_type=jnp.float32).astype(
            jnp.bfloat16
        ),
        "dp",
        scatter_dimension=0,
        tiled=True,
    )
    gate_grad = summed[None]
    return (fwd_next, bwd_next, gate_grad)


def solution(mesh):
    return jax.shard_map(
        per_device,
        mesh=mesh,
        in_specs=(
            P("pipe", ("expert", "dp"), None),
            P("pipe", ("expert", "dp"), None),
            P("pipe", ("expert", "dp"), None),
            P("pipe", ("expert", "dp"), None),
            P("pipe", ("expert", "dp"), None),
            P("pipe", ("expert", "dp"), None),
            P("pipe", ("expert", "dp"), None),
            P("pipe", "dp", "expert"),
            P("pipe", "dp", "expert"),
            P("pipe", "dp", "expert"),
        ),
        out_specs=(
            P("pipe", ("expert", "dp"), None),
            P("pipe", ("expert", "dp"), None),
            P("pipe", "dp", "expert"),
        ),
        check_vma=False,
    )
```

profile of v0, /device:TPU:1, one launch (start us, length us, event | category | flops | bytes accessed | tf_op | source)
XLA Modules:
  0.0 348.3 jit_solution(5725379315154069737)
XLA Ops:
  10.3 2.2 scatter_custom_fusion
  12.5 1.7 broadcast_in_dim.8
  14.2 9.1 %all-to-all-start = ((bf16[8,40,3584]{2,1,0:T(8,128)(2,1)}), bf16[8,40,3584]{2,1,0:T(8,128)(2,1)}, u32[]{:S(2)}, u32[]{:S(2)}) async-start(bf16[8,40,3584]{2,1,0:T(8,128)(2,1)} %bitcast.7), calls=%async_computation | async-start | bytes 4587520 | tf_op jit(solution)/shard_map/all_to_all | solution.py:95
  24.6 2.3 scatter_custom_fusion.1
  26.8 49.4 %all-to-all-done = bf16[8,40,3584]{2,1,0:T(8,128)(2,1)} async-done(((bf16[8,40,3584]{2,1,0:T(8,128)(2,1)}), bf16[8,40,3584]{2,1,0:T(8,128)(2,1)}, u32[]{:S(2)}, u32[]{:S(2)}) %all-to-all-start) | async-done | bytes 2293792 | tf_op jit(solution)/shard_map/all_to_all | solution.py:95
  76.3 1.7 broadcast_in_dim.9
  77.9 4.4 %all-to-all-start.2 = ((bf16[8,40,3584]{2,1,0:T(8,128)(2,1)}), bf16[8,40,3584]{2,1,0:T(8,128)(2,1)}, u32[]{:S(2)}, u32[]{:S(2)}) async-start(bf16[8,40,3584]{2,1,0:T(8,128)(2,1)} %bitcast.23), calls=%async_computation.2 | async-start | bytes 4587520 | tf_op jit(solution)/shard_map/all_to_all | solution.py:105
  83.1 2.2 scatter_custom_fusion.2
  85.3 50.5 %all-to-all-done.2 = bf16[8,40,3584]{2,1,0:T(8,128)(2,1)} async-done(((bf16[8,40,3584]{2,1,0:T(8,128)(2,1)}), bf16[8,40,3584]{2,1,0:T(8,128)(2,1)}, u32[]{:S(2)}, u32[]{:S(2)}) %all-to-all-start.2) | async-done | bytes 2293792 | tf_op jit(solution)/shard_map/all_to_all | solution.py:105
  135.8 1.5 broadcast_in_dim.10
  137.3 3.6 %all-to-all-start.3 = ((bf16[8,40,3584]{2,1,0:T(8,128)(2,1)}), bf16[8,40,3584]{2,1,0:T(8,128)(2,1)S(1)}, u32[]{:S(2)}, u32[]{:S(2)}) async-start(bf16[8,40,3584]{2,1,0:T(8,128)(2,1)} %bitcast.27), calls=%async_computation.3 | async-start | bytes 4587520 | tf_op jit(solution)/shard_map/all_to_all | solution.py:104
  141.0 4.5 %fusion.13 = f32[320,512]{1,0:T(8,128)S(1)} fusion(bf16[320,3584]{1,0:T(8,128)(2,1)} %bitcast.8, bf16[1,3584,512]{2,1,0:T(8,128)(2,1)} %all-gather.7.cloned.1.call-done), kind=kOutput, calls=%fused_computation.23 | convolution fusion | flops 1174405120 | bytes 6619136 | tf_op jit(solution)/shard_map/dot_general | solution.py:43
  145.5 43.1 %all-gather.9.cloned.1.call-done = bf16[1,3584,512]{2,1,0:T(8,128)(2,1)} async-done(((bf16[1,1792,512]{2,1,0:T(8,128)(2,1)}), bf16[1,3584,512]{2,1,0:T(8,128)(2,1)}) %all-gather.9.cloned.1.call-update) | async-done | bytes 3670032 | tf_op jit(solution)/shard_map/all_gather | solution.py:77
  188.6 7.9 %convolution_convert_fusion.1 = bf16[320,3584]{1,0:T(8,128)(2,1)} fusion(bf16[1,3584,512]{2,1,0:T(8,128)(2,1)} %all-gather.11.cloned.1.call-done, bf16[320,3584]{1,0:T(8,128)(2,1)} %bitcast.8, bf16[1,3584,512]{2,1,0:T(8,128)(2,1)} %all-gather.9.cloned.1.call-done, f32[320,512]{1,0:T(8,128)S(1)} %fusion.13), kind=kOutput, calls=%fused_computation.8 | convolution fusion | flops 2350940160 | bytes 12582912 | tf_op jit(solution)/shard_map/dot_general | solution.py:46
  198.1 6.5 %all-to-all-start.1 = ((bf16[8,40,3584]{2,1,0:T(8,128)(2,1)}), bf16[8,40,3584]{2,1,0:T(8,128)(2,1)S(1)}, u32[]{:S(2)}, u32[]{:S(2)}) async-start(bf16[8,40,3584]{2,1,0:T(8,128)(2,1)} %bitcast.107), calls=%async_computation.1 | async-start | bytes 4587520 | tf_op jit(solution)/shard_map/all_to_all | solution.py:96
  204.9 4.2 %fusion.1 = f32[320,512]{1,0:T(8,128)S(1)} fusion(bf16[320,3584]{1,0:T(8,128)(2,1)} %bitcast.24, bf16[1,3584,512]{2,1,0:T(8,128)(2,1)} %all-gather.11.cloned.1.call-done), kind=kOutput, calls=%fused_computation.11 | convolution fusion | flops 1174405120 | bytes 6619136 | tf_op jit(solution)/shard_map/dot_general | solution.py:60
  212.9 4.0 %convolution_convert_fusion = bf16[3584,512]{1,0:T(8,128)(2,1)} fusion(bf16[320,3584]{1,0:T(8,128)(2,1)S(1)} %bitcast.110, bf16[320,512]{1,0:T(8,128)(2,1)S(1)} %fusion.32), kind=kOutput, calls=%fused_computation.5 | convolution fusion | flops 1176240128 | bytes 6291456 | tf_op jit(solution)/shard_map/dot_general | solution.py:120
  216.9 3.6 %fusion.9 = f32[320,3584]{1,0:T(8,128)S(1)} fusion(bf16[320,512]{1,0:T(8,128)(2,1)S(1)} %fusion.32, bf16[1,3584,512]{2,1,0:T(8,128)(2,1)} %all-gather.7.cloned.1.call-done), kind=kOutput, calls=%fused_computation.19 | convolution fusion | flops 1174405120 | bytes 8585216 | tf_op jit(solution)/shard_map/dot_general | solution.py:64
  220.5 2.8 fusion
  223.3 34.1 %all-to-all-done.1 = bf16[8,40,3584]{2,1,0:T(8,128)(2,1)S(1)} async-done(((bf16[8,40,3584]{2,1,0:T(8,128)(2,1)}), bf16[8,40,3584]{2,1,0:T(8,128)(2,1)S(1)}, u32[]{:S(2)}, u32[]{:S(2)}) %all-to-all-start.1) | async-done | bytes 2293792 | tf_op jit(solution)/shard_map/all_to_all | solution.py:96
  258.8 4.4 %all-to-all-start.4 = ((bf16[8,40,3584]{2,1,0:T(8,128)(2,1)}), bf16[8,40,3584]{2,1,0:T(8,128)(2,1)}, u32[]{:S(2)}, u32[]{:S(2)}) async-start(bf16[8,40,3584]{2,1,0:T(8,128)(2,1)} %bitcast.29), calls=%async_computation.4 | async-start | bytes 4587520 | tf_op jit(solution)/shard_map/all_to_all | solution.py:108
  263.2 2.3 convert_reduce_fusion.1
  265.5 2.4 gather_fusion
  267.9 2.7 fusion.19
  270.6 4.7 %collective-permute-start = (bf16[1,128,3584]{2,1,0:T(8,128)(2,1)}, bf16[1,128,3584]{2,1,0:T(8,128)(2,1)}, u32[]{:S(2)}, u32[]{:S(2)}) collective-permute-start(bf16[1,128,3584]{2,1,0:T(8,128)(2,1)} %fusion.19), channel_id=1, source_target_pairs={{240,0},{0,16},{16,32},{32,48},{48,64},{64,80},{80,96},{96,112},{1... | collective-permute-start | bytes 2752520 | tf_op jit(solution)/shard_map/ppermute | solution.py:12
  275.3 41.4 %all-to-all-done.4 = bf16[8,40,3584]{2,1,0:T(8,128)(2,1)} async-done(((bf16[8,40,3584]{2,1,0:T(8,128)(2,1)}), bf16[8,40,3584]{2,1,0:T(8,128)(2,1)}, u32[]{:S(2)}, u32[]{:S(2)}) %all-to-all-start.4) | async-done | bytes 2293792 | tf_op jit(solution)/shard_map/all_to_all | solution.py:108
  316.7 2.3 convert_reduce_fusion
  319.0 2.4 gather_fusion.1
  321.4 2.0 fusion.15
  323.4 3.1 collective-permute-start.1
  326.5 12.2 %collective-permute-done.1 = bf16[1,128,3584]{2,1,0:T(8,128)(2,1)S(1)} collective-permute-done((bf16[1,128,3584]{2,1,0:T(8,128)(2,1)S(1)}, bf16[1,128,3584]{2,1,0:T(8,128)(2,1)S(1)}, u32[]{:S(2)}, u32[]{:S(2)}) %collective-permute-start.1) | collective-permute-done | bytes 917536 | tf_op jit(solution)/shard_map/ppermute | solution.py:12
  338.7 2.2 copy.15
  (58 shorter events, 12.9 us)
Async XLA Ops:
  7.2 75.9 %copy-start = (bf16[1,128,3584]{2,1,0:T(8,128)(2,1)S(1)}, bf16[1,128,3584]{2,1,0:T(8,128)(2,1)}, u32[]{:S(2)}) copy-start(bf16[1,128,3584]{2,1,0:T(8,128)(2,1)} %param.13) | copy-start | bytes 2752516
  7.2 3.2 copy-start.5
  7.2 133.8 %all-gather.7.cloned.1.call-start = ((), (), s32[]{:S(2)}) async-start(), calls=%async_computation.7 | async-start | bytes 5505024 | tf_op jit(solution)/shard_map/all_gather | solution.py:76
  14.2 9.9 %copy-start.13 = (s32[1,128,1]{1,2,0:T(1,128)S(1)}, s32[1,128,1]{1,2,0:T(1,128)}, u32[]{:S(2)}) copy-start(s32[1,128,1]{1,2,0:T(1,128)} %param.15) | copy-start | bytes 1540
  14.2 10.4 %copy-start.3 = (bf16[1,128,3584]{2,1,0:T(8,128)(2,1)S(1)}, bf16[1,128,3584]{2,1,0:T(8,128)(2,1)}, u32[]{:S(2)}) copy-start(bf16[1,128,3584]{2,1,0:T(8,128)(2,1)} %param.14) | copy-start | bytes 2752516
  14.2 10.4 %copy-start.14 = (f32[1,128,1]{1,2,0:T(1,128)S(1)}, f32[1,128,1]{1,2,0:T(1,128)}, u32[]{:S(2)}) copy-start(f32[1,128,1]{1,2,0:T(1,128)} %param.16) | copy-start | bytes 1540
  14.2 62.1 %all-to-all-start = ((bf16[8,40,3584]{2,1,0:T(8,128)(2,1)}), bf16[8,40,3584]{2,1,0:T(8,128)(2,1)}, u32[]{:S(2)}, u32[]{:S(2)}) async-start(bf16[8,40,3584]{2,1,0:T(8,128)(2,1)} %bitcast.7), calls=%async_computation | async-start | bytes 4587520 | tf_op jit(solution)/shard_map/all_to_all | solution.py:95
  23.4 122.2 %all-gather.11.cloned.1.call-start = ((), (), s32[]{:S(2)}) async-start(), calls=%async_computation.9 | async-start | bytes 5505024 | tf_op jit(solution)/shard_map/all_gather | solution.py:78
  77.9 57.9 %all-to-all-start.2 = ((bf16[8,40,3584]{2,1,0:T(8,128)(2,1)}), bf16[8,40,3584]{2,1,0:T(8,128)(2,1)}, u32[]{:S(2)}, u32[]{:S(2)}) async-start(bf16[8,40,3584]{2,1,0:T(8,128)(2,1)} %bitcast.23), calls=%async_computation.2 | async-start | bytes 4587520 | tf_op jit(solution)/shard_map/all_to_all | solution.py:105
  82.3 106.3 %all-gather.9.cloned.1.call-start = ((), (), s32[]{:S(2)}) async-start(), calls=%async_computation.8 | async-start | bytes 5505024 | tf_op jit(solution)/shard_map/all_gather | solution.py:77
  137.3 59.4 %all-to-all-start.3 = ((bf16[8,40,3584]{2,1,0:T(8,128)(2,1)}), bf16[8,40,3584]{2,1,0:T(8,128)(2,1)S(1)}, u32[]{:S(2)}, u32[]{:S(2)}) async-start(bf16[8,40,3584]{2,1,0:T(8,128)(2,1)} %bitcast.27), calls=%async_computation.3 | async-start | bytes 4587520 | tf_op jit(solution)/shard_map/all_to_all | solution.py:104
  196.7 1.4 copy-start.9
  198.1 59.4 %all-to-all-start.1 = ((bf16[8,40,3584]{2,1,0:T(8,128)(2,1)}), bf16[8,40,3584]{2,1,0:T(8,128)(2,1)S(1)}, u32[]{:S(2)}, u32[]{:S(2)}) async-start(bf16[8,40,3584]{2,1,0:T(8,128)(2,1)} %bitcast.107), calls=%async_computation.1 | async-start | bytes 4587520 | tf_op jit(solution)/shard_map/all_to_all | solution.py:96
  204.6 134.1 %reduce-scatter.2.cloned.1.call-start = ((), (), s32[]{:S(2)}) async-start(), calls=%async_computation.6 | async-start | bytes 5505024 | tf_op jit(solution)/shard_map/reduce_scatter | solution.py:119
  204.9 4.2 %copy-start.4 = (bf16[1,3584,512]{2,1,0:T(8,128)(2,1)S(1)}, bf16[1,3584,512]{2,1,0:T(8,128)(2,1)}, u32[]{:S(2)}) copy-start(bf16[1,3584,512]{2,1,0:T(8,128)(2,1)} %all-gather.7.cloned.1.call-done) | copy-start | bytes 11010052
  204.9 4.5 %copy-start.10 = (bf16[8,40,3584]{2,1,0:T(8,128)(2,1)S(1)}, bf16[8,40,3584]{2,1,0:T(8,128)(2,1)}, u32[]{:S(2)}) copy-start(bf16[8,40,3584]{2,1,0:T(8,128)(2,1)} %copy-done.9) | copy-start | bytes 6881284
  209.4 2.0 copy-start.7
  211.4 1.5 copy-start.11
  216.9 3.6 %copy-start.8 = (bf16[1,3584,512]{2,1,0:T(8,128)(2,1)S(1)}, bf16[1,3584,512]{2,1,0:T(8,128)(2,1)}, u32[]{:S(2)}) copy-start(bf16[1,3584,512]{2,1,0:T(8,128)(2,1)} %all-gather.9.cloned.1.call-done) | copy-start | bytes 11010052
  216.9 3.6 %copy-start.12 = (f32[320,512]{1,0:T(8,128)S(1)}, f32[320,512]{1,0:T(8,128)}, u32[]{:S(2)}) copy-start(f32[320,512]{1,0:T(8,128)} %copy-done.11) | copy-start | bytes 1966084
  257.4 1.4 copy-start.2
  258.8 57.9 %all-to-all-start.4 = ((bf16[8,40,3584]{2,1,0:T(8,128)(2,1)}), bf16[8,40,3584]{2,1,0:T(8,128)(2,1)}, u32[]{:S(2)}, u32[]{:S(2)}) async-start(bf16[8,40,3584]{2,1,0:T(8,128)(2,1)} %bitcast.29), calls=%async_computation.4 | async-start | bytes 4587520 | tf_op jit(solution)/shard_map/all_to_all | solution.py:108
  265.5 2.4 copy-start.6
  265.5 2.4 copy-start.15
  270.6 55.9 %collective-permute-start = (bf16[1,128,3584]{2,1,0:T(8,128)(2,1)}, bf16[1,128,3584]{2,1,0:T(8,128)(2,1)}, u32[]{:S(2)}, u32[]{:S(2)}) collective-permute-start(bf16[1,128,3584]{2,1,0:T(8,128)(2,1)} %fusion.19), channel_id=1, source_target_pairs={{240,0},{0,16},{16,32},{32,48},{48,64},{64,80},{80,96},{96,112},{1... | collective-permute-start | bytes 2752520 | tf_op jit(solution)/shard_map/ppermute | solution.py:12
  321.4 20.4 %copy-start.1 = (bf16[1,128,3584]{2,1,0:T(8,128)(2,1)S(1)}, bf16[1,128,3584]{2,1,0:T(8,128)(2,1)}, u32[]{:S(2)}) copy-start(bf16[1,128,3584]{2,1,0:T(8,128)(2,1)} %param.13) | copy-start | bytes 2752516
  323.4 15.3 %collective-permute-start.1 = (bf16[1,128,3584]{2,1,0:T(8,128)(2,1)S(1)}, bf16[1,128,3584]{2,1,0:T(8,128)(2,1)S(1)}, u32[]{:S(2)}, u32[]{:S(2)}) collective-permute-start(bf16[1,128,3584]{2,1,0:T(8,128)(2,1)S(1)} %fusion.15), channel_id=1, source_target_pairs={{16,0},{32,16},{48,32},{64,48},{80,64},{96,80},{112,96},{128,112},... | collective-permute-start | bytes 2752520 | tf_op jit(solution)/shard_map/ppermute | solution.py:12
Sparse Core Ops, SparseCore 0:
  9.8 61.2 all-gather.6
  72.9 56.9 all-gather.10
  131.7 56.9 all-gather.8
  217.0 55.4 reduce-scatter.1
where the time goes:
time: 349 us; the launch traced here: 348 us
  waiting for transfers between devices  233 us (67%)
  starting transfers between devices  36.2 us (10%)
  matrix products  29.8 us (9%)
  local copies, waits for them, and re-layouts  20.9 us (6%)
  other arithmetic  14.3 us (4%)
  between operations  14 us (4%)
    all_to_all x1, waiting for transfers between devices, per_device(): lax.all_to_all(z_buf, 'expert', split_axis=0, concat_axis=0, tiled=True)  50.5 us
    all_to_all x1, waiting for transfers between devices, per_device(): lax.all_to_all(f_buf, 'expert', split_axis=0, concat_axis=0, tiled=True)  49.4 us
    all_gather x1, waiting for transfers between devices, per_device(): lax.all_gather(up_w[0], 'dp', axis=0, tiled=True)  43.1 us
    all_to_all x1, waiting for transfers between devices, per_device(): lax.all_to_all(back, 'expert', split_axis=0, concat_axis=0, tiled=True)  41.4 us
    all_to_all x1, waiting for transfers between devices, per_device(): lax.all_to_all(expert_forward(received, w_gate, w_up, w_down), 'expert',...  34.1 us
    ppermute x2, waiting for transfers between devices, shifted(): return lax.ppermute(block, axis, route)  12.2 us
    all_to_all x1, starting transfers between devices, per_device(): lax.all_to_all(f_buf, 'expert', split_axis=0, concat_axis=0, tiled=True)  9.15 us
    dot_general x1, matrix products, expert_forward(): lax.dot_general(hidden, w_down, (((1,), (1,)), ((), ())), preferred_eleme...  7.94 us
  transfers between devices with their start and end apart: 11, of which 7 were waited for; matrix products, arithmetic and copies ran while one was open for 17% of the time, Pallas kernels for 0%

commit v1 on v0

--- a/solution.py
+++ b/solution.py
@@ -74,7 +74,7 @@
     experts = holders // SPLIT
     w_gate, w_up, w_down = (
         lax.all_gather(gate_w[0], "dp", axis=0, tiled=True),
-        lax.all_gather(up_w[0], "dp", axis=0, tiled=True),
+        jnp.concatenate(lax.all_to_all(jnp.stack([up_w[0]] * lax.axis_size("dp")), "dp", 0, 0), 0),
         lax.all_gather(down_w[0], "dp", axis=0, tiled=True),
     )
     f_rows = fwd_in[0]

time: 349 us -> 397 us (1.14)
  waiting for transfers between devices: 233 us -> 269 us
  starting transfers between devices: 36.2 us -> 41.5 us
    all_to_all x1, waiting for transfers between devices: 0.15 us -> 43.8 us  [per_device(): lax.all_to_all(x_buf, 'expert', split_axis=0, concat_axis=0, tiled=True)]
    all_gather x1 -> x0, waiting for transfers between devices: 43.1 us -> none  [per_device(): lax.all_gather(up_w[0], 'dp', axis=0, tiled=True)]
    all_to_all x0 -> x1, waiting for transfers between devices: none -> 38.6 us  [per_device(): lax.all_to_all(jnp.stack([up_w[0]] * lax.axis_size('dp')), 'dp', 0, 0)]
    all_to_all x0 -> x1, starting transfers between devices: none -> 5.54 us  [per_device(): lax.all_to_all(jnp.stack([up_w[0]] * lax.axis_size('dp')), 'dp', 0, 0)]
    all_to_all x1, waiting for transfers between devices: 34.1 us -> 29.5 us  [per_device(): lax.all_to_all(expert_forward(received, w_gate, w_up, w_down), 'expert',...]
    another operation x0 -> x1, other arithmetic: none -> 4.3 us  [per_device(): jnp.stack([up_w[0]] * lax.axis_size('dp'))]
  transfers between devices with their start and end apart: 11 -> 11, of which waited for: 7 -> 7; matrix products, arithmetic and copies ran while one was open for 17% -> 15% of each run, Pallas kernels for 0% -> 0%
where the time goes in v1:
time: 397 us; the launch traced here: 396 us
  waiting for transfers between devices  269 us (68%)
  starting transfers between devices  41.5 us (10%)
  matrix products  33.5 us (8%)
  local copies, waits for them, and re-layouts  21.2 us (5%)
  other arithmetic  16.8 us (4%)
  between operations  14 us (4%)
    all_to_all x1, waiting for transfers between devices, per_device(): lax.all_to_all(f_buf, 'expert', split_axis=0, concat_axis=0, tiled=True)  52.5 us
    all_to_all x1, waiting for transfers between devices, per_device(): lax.all_to_all(z_buf, 'expert', split_axis=0, concat_axis=0, tiled=True)  49.6 us
    all_to_all x1, waiting for transfers between devices, per_device(): lax.all_to_all(x_buf, 'expert', split_axis=0, concat_axis=0, tiled=True)  43.8 us
    all_to_all x1, waiting for transfers between devices, per_device(): lax.all_to_all(back, 'expert', split_axis=0, concat_axis=0, tiled=True)  41.5 us
    all_to_all x1, waiting for transfers between devices, per_device(): lax.all_to_all(jnp.stack([up_w[0]] * lax.axis_size('dp')), 'dp', 0, 0)  38.6 us
    all_to_all x1, waiting for transfers between devices, per_device(): lax.all_to_all(expert_forward(received, w_gate, w_up, w_down), 'expert',...  29.5 us
    ppermute x2, waiting for transfers between devices, shifted(): return lax.ppermute(block, axis, route)  12.3 us
    all_to_all x1, starting transfers between devices, per_device(): lax.all_to_all(f_buf, 'expert', split_axis=0, concat_axis=0, tiled=True)  10.6 us
  transfers between devices with their start and end apart: 11, of which 7 were waited for; matrix products, arithmetic and copies ran while one was open for 15% of the time, Pallas kernels for 0%

profile of v1, /device:TPU:1, one launch (start us, length us, event | category | flops | bytes accessed | tf_op | source)
XLA Modules:
  0.0 396.2 jit_solution(2660501097905261238)
XLA Ops:
  7.2 4.3 %pad_maximum_fusion = bf16[2,1792,512]{2,1,0:T(8,128)(2,1)} fusion(bf16[1,1792,512]{2,1,0:T(8,128)(2,1)} %param.18), kind=kLoop, calls=%fused_computation.11 | loop fusion | flops 1835008 | bytes 5505024 | tf_op jit(solution)/shard_map/stack | solution.py:77
  11.5 5.5 %all-to-all-start.1 = ((bf16[2,1792,512]{2,1,0:T(8,128)(2,1)}), bf16[2,1792,512]{2,1,0:T(8,128)(2,1)}, u32[]{:S(2)}, u32[]{:S(2)}) async-start(bf16[2,1792,512]{2,1,0:T(8,128)(2,1)} %pad_maximum_fusion), calls=%async_computation.1 | async-start | bytes 7340032 | tf_op jit(solution)/shard_map/all_to_all | solution.py:77
  17.5 2.2 scatter_custom_fusion
  19.7 38.6 %all-to-all-done.1 = bf16[2,1792,512]{2,1,0:T(8,128)(2,1)} async-done(((bf16[2,1792,512]{2,1,0:T(8,128)(2,1)}), bf16[2,1792,512]{2,1,0:T(8,128)(2,1)}, u32[]{:S(2)}, u32[]{:S(2)}) %all-to-all-start.1) | async-done | bytes 3670048 | tf_op jit(solution)/shard_map/all_to_all | solution.py:77
  59.9 10.6 %all-to-all-start = ((bf16[8,40,3584]{2,1,0:T(8,128)(2,1)}), bf16[8,40,3584]{2,1,0:T(8,128)(2,1)}, u32[]{:S(2)}, u32[]{:S(2)}) async-start(bf16[8,40,3584]{2,1,0:T(8,128)(2,1)} %bitcast.7), calls=%async_computation | async-start | bytes 4587520 | tf_op jit(solution)/shard_map/all_to_all | solution.py:95
  71.7 2.3 scatter_custom_fusion.1
  74.0 52.5 %all-to-all-done = bf16[8,40,3584]{2,1,0:T(8,128)(2,1)} async-done(((bf16[8,40,3584]{2,1,0:T(8,128)(2,1)}), bf16[8,40,3584]{2,1,0:T(8,128)(2,1)}, u32[]{:S(2)}, u32[]{:S(2)}) %all-to-all-start) | async-done | bytes 2293792 | tf_op jit(solution)/shard_map/all_to_all | solution.py:95
  128.1 4.4 %all-to-all-start.3 = ((bf16[8,40,3584]{2,1,0:T(8,128)(2,1)}), bf16[8,40,3584]{2,1,0:T(8,128)(2,1)}, u32[]{:S(2)}, u32[]{:S(2)}) async-start(bf16[8,40,3584]{2,1,0:T(8,128)(2,1)} %bitcast.23), calls=%async_computation.3 | async-start | bytes 4587520 | tf_op jit(solution)/shard_map/all_to_all | solution.py:105
  133.3 2.2 scatter_custom_fusion.2
  135.5 49.6 %all-to-all-done.3 = bf16[8,40,3584]{2,1,0:T(8,128)(2,1)} async-done(((bf16[8,40,3584]{2,1,0:T(8,128)(2,1)}), bf16[8,40,3584]{2,1,0:T(8,128)(2,1)}, u32[]{:S(2)}, u32[]{:S(2)}) %all-to-all-start.3) | async-done | bytes 2293792 | tf_op jit(solution)/shard_map/all_to_all | solution.py:105
  186.6 4.8 %all-to-all-start.4 = ((bf16[8,40,3584]{2,1,0:T(8,128)(2,1)}), bf16[8,40,3584]{2,1,0:T(8,128)(2,1)S(1)}, u32[]{:S(2)}, u32[]{:S(2)}) async-start(bf16[8,40,3584]{2,1,0:T(8,128)(2,1)} %bitcast.27), calls=%async_computation.4 | async-start | bytes 4587520 | tf_op jit(solution)/shard_map/all_to_all | solution.py:104
  191.4 4.1 %fusion.8 = f32[320,512]{1,0:T(8,128)S(1)} fusion(bf16[320,3584]{1,0:T(8,128)(2,1)} %bitcast.8, bf16[1,3584,512]{2,1,0:T(8,128)(2,1)} %all-gather.5.cloned.1.call-done), kind=kOutput, calls=%fused_computation.19 | convolution fusion | flops 1174405120 | bytes 6619136 | tf_op jit(solution)/shard_map/dot_general | solution.py:43
  195.5 7.9 %convolution_convert_fusion.1 = bf16[320,3584]{1,0:T(8,128)(2,1)} fusion(bf16[1,3584,512]{2,1,0:T(8,128)(2,1)} %all-gather.7.cloned.1.call-done, bf16[320,3584]{1,0:T(8,128)(2,1)} %bitcast.8, bf16[3584,512]{1,0:T(8,128)(2,1)} %bitcast.10, f32[320,512]{1,0:T(8,128)S(1)} %fusion.8), kind=kOutput, calls=%fused_computation.8 | convolution fusion | flops 2350940160 | bytes 12582912 | tf_op jit(solution)/shard_map/dot_general | solution.py:46
  203.5 43.8 %all-to-all-done.4 = bf16[8,40,3584]{2,1,0:T(8,128)(2,1)S(1)} async-done(((bf16[8,40,3584]{2,1,0:T(8,128)(2,1)}), bf16[8,40,3584]{2,1,0:T(8,128)(2,1)S(1)}, u32[]{:S(2)}, u32[]{:S(2)}) %all-to-all-start.4) | async-done | bytes 2293792 | tf_op jit(solution)/shard_map/all_to_all | solution.py:104
  248.6 3.6 all-to-all-start.2
  252.5 4.2 %fusion.1 = f32[320,512]{1,0:T(8,128)S(1)} fusion(bf16[320,3584]{1,0:T(8,128)(2,1)} %bitcast.24, bf16[1,3584,512]{2,1,0:T(8,128)(2,1)} %all-gather.7.cloned.1.call-done), kind=kOutput, calls=%fused_computation.12 | convolution fusion | flops 1174405120 | bytes 6619136 | tf_op jit(solution)/shard_map/dot_general | solution.py:60
  259.2 3.5 fusion.18
  262.7 4.0 %convolution_convert_fusion = bf16[3584,512]{1,0:T(8,128)(2,1)} fusion(bf16[320,3584]{1,0:T(8,128)(2,1)S(1)} %bitcast.93, bf16[320,512]{1,0:T(8,128)(2,1)S(1)} %fusion.18), kind=kOutput, calls=%fused_computation.5 | convolution fusion | flops 1176240128 | bytes 6291456 | tf_op jit(solution)/shard_map/dot_general | solution.py:120
  266.8 3.5 fusion.4
  270.3 4.9 %fusion = bf16[320,3584]{1,0:T(8,128)(2,1)} fusion(f32[320,3584]{1,0:T(8,128)S(1)} %fusion.4, bf16[3584,512]{1,0:T(8,128)(2,1)} %bitcast.10, f32[320,512]{1,0:T(8,128)S(1)} %fusion.1, f32[320,512]{1,0:T(8,128)S(1)} %copy-done.10), kind=kOutput, calls=%fused_computation.7 | convolution fusion | flops 1177681920 | bytes 11862016 | tf_op jit(solution)/shard_map/dot_general | solution.py:65
  275.1 29.5 %all-to-all-done.2 = bf16[8,40,3584]{2,1,0:T(8,128)(2,1)S(1)} async-done(((bf16[8,40,3584]{2,1,0:T(8,128)(2,1)}), bf16[8,40,3584]{2,1,0:T(8,128)(2,1)S(1)}, u32[]{:S(2)}, u32[]{:S(2)}) %all-to-all-start.2) | async-done | bytes 2293792 | tf_op jit(solution)/shard_map/all_to_all | solution.py:96
  306.2 4.8 %all-to-all-start.5 = ((bf16[8,40,3584]{2,1,0:T(8,128)(2,1)}), bf16[8,40,3584]{2,1,0:T(8,128)(2,1)}, u32[]{:S(2)}, u32[]{:S(2)}) async-start(bf16[8,40,3584]{2,1,0:T(8,128)(2,1)} %bitcast.29), calls=%async_computation.5 | async-start | bytes 4587520 | tf_op jit(solution)/shard_map/all_to_all | solution.py:108
  311.0 2.4 convert_reduce_fusion.1
  313.4 2.4 gather_fusion
  315.9 2.7 fusion.14
  318.6 4.5 %collective-permute-start = (bf16[1,128,3584]{2,1,0:T(8,128)(2,1)}, bf16[1,128,3584]{2,1,0:T(8,128)(2,1)}, u32[]{:S(2)}, u32[]{:S(2)}) collective-permute-start(bf16[1,128,3584]{2,1,0:T(8,128)(2,1)} %fusion.14), channel_id=1, source_target_pairs={{240,0},{0,16},{16,32},{32,48},{48,64},{64,80},{80,96},{96,112},{1... | collective-permute-start | bytes 2752520 | tf_op jit(solution)/shard_map/ppermute | solution.py:12
  323.1 41.5 %all-to-all-done.5 = bf16[8,40,3584]{2,1,0:T(8,128)(2,1)} async-done(((bf16[8,40,3584]{2,1,0:T(8,128)(2,1)}), bf16[8,40,3584]{2,1,0:T(8,128)(2,1)}, u32[]{:S(2)}, u32[]{:S(2)}) %all-to-all-start.5) | async-done | bytes 2293792 | tf_op jit(solution)/shard_map/all_to_all | solution.py:108
  364.6 2.3 convert_reduce_fusion
  366.9 2.4 gather_fusion.1
  371.3 3.0 collective-permute-start.1
  374.3 12.3 %collective-permute-done.1 = bf16[1,128,3584]{2,1,0:T(8,128)(2,1)S(1)} collective-permute-done((bf16[1,128,3584]{2,1,0:T(8,128)(2,1)S(1)}, bf16[1,128,3584]{2,1,0:T(8,128)(2,1)S(1)}, u32[]{:S(2)}, u32[]{:S(2)}) %collective-permute-start.1) | collective-permute-done | bytes 917536 | tf_op jit(solution)/shard_map/ppermute | solution.py:12
  386.6 2.2 copy.15
  (56 shorter events, 15.7 us)
Async XLA Ops:
  7.2 126.1 %copy-start = (bf16[1,128,3584]{2,1,0:T(8,128)(2,1)S(1)}, bf16[1,128,3584]{2,1,0:T(8,128)(2,1)}, u32[]{:S(2)}) copy-start(bf16[1,128,3584]{2,1,0:T(8,128)(2,1)} %param.13) | copy-start | bytes 2752516
  11.5 5.6 %copy-start.11 = (s32[1,128,1]{1,2,0:T(1,128)S(1)}, s32[1,128,1]{1,2,0:T(1,128)}, u32[]{:S(2)}) copy-start(s32[1,128,1]{1,2,0:T(1,128)} %param.11) | copy-start | bytes 1540
  11.5 6.0 %copy-start.5 = (bf16[1,128,3584]{2,1,0:T(8,128)(2,1)S(1)}, bf16[1,128,3584]{2,1,0:T(8,128)(2,1)}, u32[]{:S(2)}) copy-start(bf16[1,128,3584]{2,1,0:T(8,128)(2,1)} %param.10) | copy-start | bytes 2752516
  11.5 46.8 %all-to-all-start.1 = ((bf16[2,1792,512]{2,1,0:T(8,128)(2,1)}), bf16[2,1792,512]{2,1,0:T(8,128)(2,1)}, u32[]{:S(2)}, u32[]{:S(2)}) async-start(bf16[2,1792,512]{2,1,0:T(8,128)(2,1)} %pad_maximum_fusion), calls=%async_computation.1 | async-start | bytes 7340032 | tf_op jit(solution)/shard_map/all_to_all | solution.py:77
  59.9 11.3 %copy-start.12 = (s32[1,128,1]{1,2,0:T(1,128)S(1)}, s32[1,128,1]{1,2,0:T(1,128)}, u32[]{:S(2)}) copy-start(s32[1,128,1]{1,2,0:T(1,128)} %param.15) | copy-start | bytes 1540
  59.9 11.8 %copy-start.3 = (bf16[1,128,3584]{2,1,0:T(8,128)(2,1)S(1)}, bf16[1,128,3584]{2,1,0:T(8,128)(2,1)}, u32[]{:S(2)}) copy-start(bf16[1,128,3584]{2,1,0:T(8,128)(2,1)} %param.14) | copy-start | bytes 2752516
  59.9 11.8 %copy-start.13 = (f32[1,128,1]{1,2,0:T(1,128)S(1)}, f32[1,128,1]{1,2,0:T(1,128)}, u32[]{:S(2)}) copy-start(f32[1,128,1]{1,2,0:T(1,128)} %param.16) | copy-start | bytes 1540
  59.9 66.5 %all-to-all-start = ((bf16[8,40,3584]{2,1,0:T(8,128)(2,1)}), bf16[8,40,3584]{2,1,0:T(8,128)(2,1)}, u32[]{:S(2)}, u32[]{:S(2)}) async-start(bf16[8,40,3584]{2,1,0:T(8,128)(2,1)} %bitcast.7), calls=%async_computation | async-start | bytes 4587520 | tf_op jit(solution)/shard_map/all_to_all | solution.py:95
  70.5 120.9 %all-gather.5.cloned.1.call-start = ((), (), s32[]{:S(2)}) async-start(), calls=%async_computation.8 | async-start | bytes 5505024 | tf_op jit(solution)/shard_map/all_gather | solution.py:76
  128.1 56.9 %all-to-all-start.3 = ((bf16[8,40,3584]{2,1,0:T(8,128)(2,1)}), bf16[8,40,3584]{2,1,0:T(8,128)(2,1)}, u32[]{:S(2)}, u32[]{:S(2)}) async-start(bf16[8,40,3584]{2,1,0:T(8,128)(2,1)} %bitcast.23), calls=%async_computation.3 | async-start | bytes 4587520 | tf_op jit(solution)/shard_map/all_to_all | solution.py:105
  132.5 63.0 %all-gather.7.cloned.1.call-start = ((), (), s32[]{:S(2)}) async-start(), calls=%async_computation.9 | async-start | bytes 5505024 | tf_op jit(solution)/shard_map/all_gather | solution.py:78
  186.6 60.7 %all-to-all-start.4 = ((bf16[8,40,3584]{2,1,0:T(8,128)(2,1)}), bf16[8,40,3584]{2,1,0:T(8,128)(2,1)S(1)}, u32[]{:S(2)}, u32[]{:S(2)}) async-start(bf16[8,40,3584]{2,1,0:T(8,128)(2,1)} %bitcast.27), calls=%async_computation.4 | async-start | bytes 4587520 | tf_op jit(solution)/shard_map/all_to_all | solution.py:104
  247.3 1.4 copy-start.7
  248.6 56.0 %all-to-all-start.2 = ((bf16[8,40,3584]{2,1,0:T(8,128)(2,1)}), bf16[8,40,3584]{2,1,0:T(8,128)(2,1)S(1)}, u32[]{:S(2)}, u32[]{:S(2)}) async-start(bf16[8,40,3584]{2,1,0:T(8,128)(2,1)} %bitcast.90), calls=%async_computation.2 | async-start | bytes 4587520 | tf_op jit(solution)/shard_map/all_to_all | solution.py:96
  252.3 134.3 %reduce-scatter.2.cloned.1.call-start = ((), (), s32[]{:S(2)}) async-start(), calls=%async_computation.7 | async-start | bytes 5505024 | tf_op jit(solution)/shard_map/reduce_scatter | solution.py:119
  252.5 4.2 %copy-start.4 = (bf16[1,3584,512]{2,1,0:T(8,128)(2,1)S(1)}, bf16[1,3584,512]{2,1,0:T(8,128)(2,1)}, u32[]{:S(2)}) copy-start(bf16[1,3584,512]{2,1,0:T(8,128)(2,1)} %all-gather.5.cloned.1.call-done) | copy-start | bytes 11010052
  252.5 4.5 %copy-start.8 = (bf16[8,40,3584]{2,1,0:T(8,128)(2,1)S(1)}, bf16[8,40,3584]{2,1,0:T(8,128)(2,1)}, u32[]{:S(2)}) copy-start(bf16[8,40,3584]{2,1,0:T(8,128)(2,1)} %copy-done.7) | copy-start | bytes 6881284
  258.3 0.8 copy-start.9
  266.8 3.5 copy-start.10
  304.7 1.5 copy-start.2
  306.2 58.5 %all-to-all-start.5 = ((bf16[8,40,3584]{2,1,0:T(8,128)(2,1)}), bf16[8,40,3584]{2,1,0:T(8,128)(2,1)}, u32[]{:S(2)}, u32[]{:S(2)}) async-start(bf16[8,40,3584]{2,1,0:T(8,128)(2,1)} %bitcast.29), calls=%async_computation.5 | async-start | bytes 4587520 | tf_op jit(solution)/shard_map/all_to_all | solution.py:108
  313.4 2.5 copy-start.6
  313.4 2.4 copy-start.14
  318.6 55.7 %collective-permute-start = (bf16[1,128,3584]{2,1,0:T(8,128)(2,1)}, bf16[1,128,3584]{2,1,0:T(8,128)(2,1)}, u32[]{:S(2)}, u32[]{:S(2)}) collective-permute-start(bf16[1,128,3584]{2,1,0:T(8,128)(2,1)} %fusion.14), channel_id=1, source_target_pairs={{240,0},{0,16},{16,32},{32,48},{48,64},{64,80},{80,96},{96,112},{1... | collective-permute-start | bytes 2752520 | tf_op jit(solution)/shard_map/ppermute | solution.py:12
  369.3 20.3 %copy-start.1 = (bf16[1,128,3584]{2,1,0:T(8,128)(2,1)S(1)}, bf16[1,128,3584]{2,1,0:T(8,128)(2,1)}, u32[]{:S(2)}) copy-start(bf16[1,128,3584]{2,1,0:T(8,128)(2,1)} %param.13) | copy-start | bytes 2752516
  371.3 15.2 %collective-permute-start.1 = (bf16[1,128,3584]{2,1,0:T(8,128)(2,1)S(1)}, bf16[1,128,3584]{2,1,0:T(8,128)(2,1)S(1)}, u32[]{:S(2)}, u32[]{:S(2)}) collective-permute-start(bf16[1,128,3584]{2,1,0:T(8,128)(2,1)S(1)} %fusion.10), channel_id=1, source_target_pairs={{16,0},{32,16},{48,32},{64,48},{80,64},{96,80},{112,96},{128,112},... | collective-permute-start | bytes 2752520 | tf_op jit(solution)/shard_map/ppermute | solution.py:12
Sparse Core Ops, SparseCore 0:
  73.1 58.7 all-gather.4
  135.2 57.3 all-gather.6
  266.9 55.3 reduce-scatter.1
